TPU v7x, 32 devices: a whole 2x2x4 slice. The times are simulated.
32 devices in a mesh: dp: 1, dap: 32 (over z, y, x, core).
Axes of the slice: x: 2, y: 2, z: 4, core: 2. Of those that a mesh axis runs over, the one named last changes fastest.
Arguments:
- alignment: bfloat16 [128, 256, 256], P(('dp', 'dap')), may hold values from -6 to 6
- pair_rep: bfloat16 [256, 256, 128], P(('dp', 'dap')), may hold values from -6 to 6
- align_mask: int32 [128, 256], P(('dp', 'dap')), may hold values 0 or 1
- residue_mask: int32 [256], P('dp'), may hold values 0 or 1
- row_gain: float32 [256], replicated, may hold values from 0.1 to 1.9
- pair_gain: float32 [128], replicated, may hold values from 0.1 to 1.9
- row_bias: bfloat16 [128, 8], replicated, may hold values from -0.5 to 0.5
- row_scoring: bfloat16 [256, 512], replicated, may hold values from -4 to 4
- row_values: bfloat16 [256, 512], replicated, may hold values from -0.375 to 0.375
- row_output: bfloat16 [256, 256], replicated, may hold values from -0.375 to 0.375
- column_gain: float32 [256], replicated, may hold values from 0.1 to 1.9
- column_scoring: bfloat16 [256, 512], replicated, may hold values from -4 to 4
- column_values: bfloat16 [256, 512], replicated, may hold values from -0.375 to 0.375
- column_output: bfloat16 [256, 256], replicated, may hold values from -0.375 to 0.375
- outer_gain: float32 [256], replicated, may hold values from 0.1 to 1.9
- outer_inputs: bfloat16 [256, 64], replicated, may hold values from -0.375 to 0.375
- outer_output: bfloat16 [1024, 128], replicated, may hold values from -1 to 1
Outputs:
- new_alignment: bfloat16 [128, 256, 256], P(('dp', 'dap'))
- new_pair: bfloat16 [256, 256, 128], P(('dp', 'dap'))
All inputs are finite; a program needn't handle non-finite values. No bound on the sum of `align_mask` on one device may be relied on, other than what follows from the above.
Results may differ from a plain program's by a relative error of at most 0.012.
The roundings to bfloat16 on the way count: a program that leaves them out, or rounds other values in their place, can miss the bound.
Values may be sent and summed in bfloat16 or wider, within the bound.
A program may use at most 64 MiB of HBM per device.

v0:
```python
import functools
import math

import jax
import jax.numpy as jnp
from jax import lax
from jax.experimental import pallas as pl
from jax.experimental.pallas import tpu as pltpu
from jax.sharding import PartitionSpec as P

HEADS = 8
HEAD = 32
C_OPM = 32
LOG2E = math.log2(math.e)
SCALE = LOG2E / math.sqrt(HEAD)
MASKED = -1000000000.0 * LOG2E
NT = (((1,), (1,)), ((), ()))
MESH = pl.DeviceIdType.MESH
VMEM = pl.BlockSpec(memory_space=pltpu.VMEM)
LIMIT = 60 * 1024 * 1024


def norm(wide, gain):
    average = jnp.mean(wide, axis=-1, keepdims=True)
    centred = wide - average
    spread = jnp.mean(centred * centred, axis=-1, keepdims=True)
    return (centred * lax.rsqrt(spread + 1e-05) * gain).astype(jnp.bfloat16)


def dot(a, b):
    return jnp.dot(a, b, preferred_element_type=jnp.float32)


def dot_nt(a, b):
    return lax.dot_general(a, b, NT, preferred_element_type=jnp.float32)


def greet_all(n, me):
    barrier = pltpu.get_barrier_semaphore()

    def one(k, carry):
        pl.semaphore_signal(
            barrier, inc=1, device_id={"dap": lax.rem(me + k, n)}, device_id_type=MESH
        )
        return carry

    lax.fori_loop(1, n, one, 0)


def met_all(n):
    pl.semaphore_wait(pltpu.get_barrier_semaphore(), n - 1)


class Gather:
    def __init__(self, n, me, out, zs, zr, ps, pr, cs, cr):
        self.n, self.me, self.out = n, me, out
        self.sems = {"z": (zs, zr), "p": (ps, pr), "c": (cs, cr)}
        self.layers = n // 8
        self.z = me // 8
        self.p = lax.rem(me // 2, 4)
        self.c = lax.rem(me, 2)

    def place(self, z, p, c):
        return z * 8 + p * 2 + c

    def plane(self, p, k):
        if k == 0:
            return p
        if k == 1:
            return p + 1 - 2 * lax.rem(p, 2)
        if k == 2:
            return lax.rem(p + 2, 4)
        return 3 - p

    def copy(self, kind, slot, block, target):
        send, recv = self.sems[kind]
        return pltpu.make_async_remote_copy(
            src_ref=self.out.at[block],
            dst_ref=self.out.at[block],
            send_sem=send.at[slot],
            recv_sem=recv.at[slot],
            device_id={"dap": target},
            device_id_type=MESH,
        )

    def layer(self, d):
        return lax.rem(self.z + self.layers - d, self.layers)

    def z_copy(self, d):
        return self.copy("z", d, self.me, self.place(lax.rem(self.z + d, self.layers), self.p, self.c))

    def p_copy(self, d, k):
        block = self.place(self.layer(d), self.p, self.c)
        return self.copy("p", d * 4 + k, block, self.place(self.z, self.plane(self.p, k), self.c))

    def c_copy(self, d, k):
        block = self.place(self.layer(d), self.plane(self.p, k), self.c)
        return self.copy("c", d * 4 + k, block, self.place(self.z, self.p, 1 - self.c))

    def z_arrived(self, d):
        block = self.place(self.layer(d), self.p, self.c)
        self.copy("z", d, block, self.place(lax.rem(self.z + d, self.layers), self.p, self.c)).wait_recv()

    def p_arrived(self, d, k):
        block = self.place(self.layer(d), self.plane(self.p, k), self.c)
        self.copy("p", d * 4 + k, block, self.place(self.z, self.plane(self.p, k), self.c)).wait_recv()

    def c_arrived(self, d, k):
        block = self.place(self.layer(d), self.plane(self.p, k), 1 - self.c)
        self.copy("c", d * 4 + k, block, self.place(self.z, self.p, 1 - self.c)).wait_recv()

    def start(self):
        for d in range(1, self.layers):
            self.z_copy(d).start()
        for k in (1, 2, 3):
            self.p_copy(0, k).start()
        self.c_copy(0, 0).start()

    def relay_layers(self):
        for d in range(1, self.layers):
            self.z_arrived(d)
            for k in (1, 2, 3):
                self.p_copy(d, k).start()
            self.c_copy(d, 0).start()

    def relay_plane(self):
        for d in range(self.layers):
            for k in (1, 2, 3):
                self.p_arrived(d, k)
                self.c_copy(d, k).start()

    def finish(self):
        for d in range(self.layers):
            for k in range(4):
                self.c_arrived(d, k)
        for d in range(self.layers):
            if d > 0:
                self.z_copy(d).wait_send()
            for k in range(4):
                if k > 0:
                    self.p_copy(d, k).wait_send()
                self.c_copy(d, k).wait_send()


def gather_sems(n):
    layers = n // 8
    sizes = (layers, layers, layers * 4, layers * 4, layers * 4, layers * 4)
    return [pltpu.SemaphoreType.DMA((size,)) for size in sizes]


class Exchange:
    def __init__(self, n, me, src, dst, piece, send, recv):
        self.n, self.me, self.src, self.dst = n, me, src, dst
        self.rows, self.first = pl.ds(piece * 16, 16), piece * n
        self.send, self.recv = send, recv

    def copy(self, k, block_out, block_in):
        return pltpu.make_async_remote_copy(
            src_ref=self.src.at[block_out, self.rows],
            dst_ref=self.dst.at[block_in, self.rows],
            send_sem=self.send.at[self.first + k],
            recv_sem=self.recv.at[self.first + k],
            device_id={"dap": block_out},
            device_id_type=MESH,
        )

    def start(self):
        def one(k, carry):
            self.copy(k, lax.rem(self.me + k, self.n), self.me).start()
            return carry

        lax.fori_loop(1, self.n, one, 0)
        self.dst[self.me, self.rows] = self.src[self.me, self.rows]

    def finish(self):
        def one(k, carry):
            target = lax.rem(self.me + k, self.n)
            self.copy(k, target, lax.rem(self.me + self.n - k, self.n)).wait_recv()
            self.copy(k, target, self.me).wait_send()
            return carry

        lax.fori_loop(1, self.n, one, 0)


def attend(joint, gated, keeps, width, bias):
    queries, keys_all = joint[:, :width], joint[:, width:]
    values_all, gates = gated[:, :width], gated[:, width:]
    groups = len(keeps)
    length = joint.shape[0] // groups
    lanes = lax.broadcasted_iota(jnp.int32, (1, width), 1) // HEAD
    totals = [None] * groups
    for h in range(HEADS):
        mine = (lanes == h).astype(jnp.float32).astype(jnp.bfloat16)
        asked, given = queries * mine, values_all * mine
        for g in range(groups):
            part = slice(g * length, (g + 1) * length)
            scores = dot_nt(asked[part], keys_all[part]) * SCALE
            if bias is not None:
                scores = scores + bias(h)
            scores = jnp.where(keeps[g], scores, MASKED)
            powers = jnp.exp2(scores - jnp.max(scores, axis=-1, keepdims=True))
            weights = powers * (1.0 / jnp.sum(powers, axis=-1, keepdims=True))
            mixed = dot(weights.astype(jnp.bfloat16), given[part])
            totals[g] = mixed if totals[g] is None else totals[g] + mixed
    total = jnp.concatenate(totals, axis=0) if groups > 1 else totals[0]
    return (total * jax.nn.sigmoid(gates.astype(jnp.float32))).astype(jnp.bfloat16)


N_IN = 17


def kernel(n, *refs):
    inputs, (back, new_pair), scratch = refs[:N_IN], refs[N_IN : N_IN + 2], refs[N_IN + 2 :]
    held, scratch = scratch[:N_IN], scratch[N_IN:]
    (
        turned, every_bias, wide_bias, joints, gates, stage, sent, columns, wide, turned_right,
        new_sent, left, every_right, wide_right, products, wide_output, turned_output, in_sems,
        ex_send, ex_recv, back_send, back_recv, *sems,
    ) = scratch
    (
        alignment, pair_rep, align_mask, residue_mask, row_gain, pair_gain, row_bias, row_scoring,
        row_values, row_output, column_gain, column_scoring, column_values, column_output,
        outer_gain, outer_inputs, outer_output,
    ) = held
    narrow, full = jnp.bfloat16, jnp.float32
    me = lax.axis_index("dap")
    seqs, total_res, width = alignment.shape
    rows = pair_rep.shape[0]
    total_seqs = seqs * n
    half = rows // 2

    order = (1, 5, 6, 2, 0, 4, 7, 8, 3, 9, 10, 11, 12, 13, 14, 15, 16)
    loads = [pltpu.make_async_copy(inputs[k], held[k], in_sems.at[k]) for k in range(N_IN)]
    for k in order:
        loads[k].start()
    greet_all(n, me)

    for k in (1, 5, 6, 2):
        loads[k].wait()
    for i in range(rows):
        normed = norm(pair_rep[i].astype(full), pair_gain[...])
        turned[:HEADS, i, :] = dot_nt(row_bias[...], normed)
    turned[HEADS] = jnp.zeros(turned.shape[1:], full)
    turned[HEADS + 1] = jnp.zeros(turned.shape[1:], full)
    turned[HEADS, :seqs, :] = align_mask[...].astype(full)
    every_bias[me] = turned[...].reshape(every_bias.shape[1:]).astype(narrow)
    met_all(n)
    gather = Gather(n, me, every_bias, *sems[:6])
    gather.start()

    def project(s, carry):
        normed = norm(alignment[s].astype(full), row_gain[...])
        joints[s] = dot(normed, row_scoring[...]).astype(narrow)
        gates[s] = dot(normed, row_values[...]).astype(narrow)
        return carry

    for k in (0, 4, 7, 8):
        loads[k].wait()
    lax.fori_loop(0, seqs // 2, project, 0)
    gather.relay_layers()
    lax.fori_loop(seqs // 2, seqs, project, 0)
    gather.relay_plane()
    for k in (3, 9, 10, 11, 12, 13, 14, 15, 16):
        loads[k].wait()
    wide_output[...] = outer_output[...].astype(full).reshape(wide_output.shape)
    for g in range(C_OPM // 4):
        piece = jnp.concatenate([wide_output[:, g * 4 + t, :] for t in range(4)], axis=0)
        turned_output[:, g * 128 : (g + 1) * 128] = piece.T.astype(narrow)
    gather.finish()

    wide_bias[...] = every_bias[:, : HEADS * rows, :].astype(full) * LOG2E
    every_mask = every_bias[:, HEADS * rows :, :].astype(full)[:, :rows, :].reshape(n * rows, total_res)
    place = lax.broadcasted_iota(jnp.int32, (total_seqs, n * rows), 0)
    spot = lax.broadcasted_iota(jnp.int32, (total_seqs, n * rows), 1)
    pick = (spot == place // seqs * rows + place % seqs).astype(full).astype(narrow)
    mask = dot(pick, every_mask.astype(narrow)).astype(narrow)
    near = lax.broadcasted_iota(jnp.int32, (rows, total_res), 1) - me * rows
    own = (near == lax.broadcasted_iota(jnp.int32, (rows, total_res), 0)).astype(full)
    keep_columns = dot_nt(own.astype(narrow), mask)
    residue_float = residue_mask[...].astype(full)
    row_factor = jnp.sum(own * residue_float, axis=-1, keepdims=True)
    pair_count = dot(keep_columns.astype(narrow), mask)
    scale = row_factor * residue_float / (0.001 + pair_count)

    def bias(h):
        return wide_bias[:, h * rows : (h + 1) * rows, :].reshape(total_res, total_res)

    to_columns = []
    for piece in range(2):
        for t in range(2):
            s = piece * 2 + t
            keep = align_mask[s : s + 1, :].astype(full) * residue_float
            mixed = attend(joints[s], gates[s], [keep > 0], width, bias)
            updated = alignment[s].astype(full) + dot(mixed, row_output[...])
            stage[:, t] = updated.reshape(n, rows, width)
        sent[:, piece * 16 : (piece + 1) * 16, :] = stage[...].reshape(n, 16, width).astype(narrow)
        to_columns.append(Exchange(n, me, sent, columns, piece, ex_send, ex_recv))
        to_columns[piece].start()
    for piece in range(2):
        to_columns[piece].finish()

    wide[...] = columns[...].astype(full).reshape(wide.shape)
    backwards = []
    for piece in range(2):
        mine = range(piece * half, (piece + 1) * half)
        stream = jnp.concatenate([wide[:, i, :] for i in mine], axis=0)
        normed = norm(stream, column_gain[...])
        joint = dot(normed, column_scoring[...]).astype(narrow)
        gated = dot(normed, column_values[...]).astype(narrow)
        keeps = [keep_columns[i : i + 1, :] > 0 for i in mine]
        mixed = attend(joint, gated, keeps, width, None)
        second = (stream + dot(mixed, column_output[...])).astype(narrow).astype(full)
        outer_normed = norm(second, outer_gain[...])
        for t, i in enumerate(mine):
            part = slice(t * total_seqs, (t + 1) * total_seqs)
            sides = dot_nt(outer_inputs[...], outer_normed[part]) * keep_columns[i : i + 1, :]
            left[i] = sides[:C_OPM].astype(narrow)
            turned_right[:, i, :] = sides[C_OPM:]
            wide[:, i, :] = second[part]
        block = wide[:, piece * half : (piece + 1) * half, :].reshape(n, 16, width)
        new_sent[:, piece * 16 : (piece + 1) * 16, :] = block.astype(narrow)
        backwards.append(Exchange(n, me, new_sent, back, piece, back_send, back_recv))
        if piece == 0:
            backwards[0].start()
    every_right[me] = turned_right[...].reshape(every_right.shape[1:]).astype(narrow)
    gather = Gather(n, me, every_right, *sems[6:])
    gather.start()
    backwards[1].start()
    gather.relay_layers()
    gather.relay_plane()
    gather.finish()

    sides = left[...].reshape(rows * C_OPM, total_seqs)
    wide_right[...] = every_right[...].astype(full)
    for e in range(C_OPM):
        piece = wide_right[:, e * rows : (e + 1) * rows, :].reshape(total_res, total_seqs)
        block = dot_nt(sides, piece.astype(narrow)).astype(narrow)
        products[:, e * C_OPM : (e + 1) * C_OPM, :] = block.reshape(rows, C_OPM, total_res)
    for i in range(rows):
        flat = dot(turned_output[...], products[i]) * scale[i : i + 1, :]
        new_pair[i] = (pair_rep[i].astype(full) + flat.T).astype(narrow)
    for piece in range(2):
        backwards[piece].finish()


def body(n, alignment, pair_rep, align_mask, residue_mask, *rest):
    (
        row_gain, pair_gain, row_bias, row_scoring, row_values, row_output, column_gain,
        column_scoring, column_values, column_output, outer_gain, outer_inputs, outer_output,
    ) = rest
    seqs, total_res, width = alignment.shape
    rows, _, channels = pair_rep.shape
    total_seqs = seqs * n
    narrow, full = jnp.bfloat16, jnp.float32
    arguments = (
        alignment, pair_rep, align_mask, residue_mask[None], row_gain[None], pair_gain[None],
        row_bias.T, row_scoring, row_values, row_output, column_gain[None], column_scoring,
        column_values, column_output, outer_gain[None], outer_inputs.T, outer_output,
    )
    dma = pltpu.SemaphoreType.DMA
    blocks = (n, seqs * rows, width)
    right_shape = (C_OPM * rows, total_seqs)
    flat = C_OPM * C_OPM
    back, new_pair = pl.pallas_call(
        functools.partial(kernel, n),
        out_shape=(
            jax.ShapeDtypeStruct(blocks, narrow),
            jax.ShapeDtypeStruct(pair_rep.shape, narrow),
        ),
        in_specs=[pl.BlockSpec(memory_space=pltpu.HBM)] * N_IN,
        out_specs=(VMEM, VMEM),
        scratch_shapes=[pltpu.VMEM(array.shape, array.dtype) for array in arguments]
        + [
            pltpu.VMEM((HEADS + 2, rows, total_res), full),
            pltpu.VMEM((n, (HEADS + 2) * rows, total_res), narrow),
            pltpu.VMEM((n, HEADS * rows, total_res), full),
            pltpu.VMEM((seqs, total_res, 2 * width), narrow),
            pltpu.VMEM((seqs, total_res, 2 * width), narrow),
            pltpu.VMEM((n, 2, rows, width), full),
            pltpu.VMEM(blocks, narrow),
            pltpu.VMEM(blocks, narrow),
            pltpu.VMEM((total_seqs, rows, width), full),
            pltpu.VMEM((C_OPM, rows, total_seqs), full),
            pltpu.VMEM(blocks, narrow),
            pltpu.VMEM((rows, C_OPM, total_seqs), narrow),
            pltpu.VMEM((n,) + right_shape, narrow),
            pltpu.VMEM((n,) + right_shape, full),
            pltpu.VMEM((rows, flat, total_res), narrow),
            pltpu.VMEM((C_OPM, C_OPM, channels), full),
            pltpu.VMEM((channels, flat), narrow),
            dma((N_IN,)),
        ]
        + [dma((2 * n,))] * 4
        + gather_sems(n)
        + gather_sems(n),
        compiler_params=pltpu.CompilerParams(
            vmem_limit_bytes=LIMIT, collective_id=0, has_side_effects=True
        ),
        name="evoformer",
    )(*arguments)
    back = back.reshape(n, 2, seqs, rows // 2, width).transpose(2, 0, 1, 3, 4)
    return back.reshape(alignment.shape), new_pair


def solution(mesh):
    split = P(("dp", "dap"), None, None)
    in_specs = (split, split, P(("dp", "dap"), None), P("dp")) + (P(),) * 13
    return jax.shard_map(
        functools.partial(body, mesh.shape["dap"]),
        mesh=mesh,
        in_specs=in_specs,
        out_specs=(split, split),
        check_vma=False,
    )
```

profile of v0, /device:TPU:0, one launch (start us, length us, event | category | flops | bytes accessed | tf_op | source)
XLA Modules:
  0.0 76.2 jit_solution(10197620142255335621)
XLA Ops:
  0.6 72.4 %evoformer.1 = (bf16[32,32,256]{2,1,0:T(8,128)(2,1)}, bf16[8,256,128]{2,1,0:T(8,128)(2,1)}) custom-call(bf16[4,256,256]{2,1,0:T(8,128)(2,1)} %refs_0_.1, bf16[8,256,128]{2,1,0:T(8,128)(2,1)} %refs_1_.1, s32[4,256]{1,0:T(4,128)} %refs_2_.1, s32[1,256]{1,0:T(1,128)} %bitcast.11, f32[1,256]{1,0:T(1,128)} %bitcast.12, f32[1,128]{1,0:T(1,128)} %bitcast.15, ...), custom_call_target="tpu_custom_call" | custom-call | tf_op jit(solution)/shard_map/evoformer/pallas_call | solution.py:364
  73.0 1.2 %reshape.10 = bf16[32,2,4,4,256]{4,3,2,1,0:T(4,128)(2,1)S(1)} reshape(bf16[32,32,256]{2,1,0:T(8,128)(2,1)} %get-tuple-element.4) | data formatting | bytes 1048576 | tf_op jit(solution)/shard_map/reshape | solution.py:401
  74.2 0.2 copy.19
  74.4 0.0 copy-start
  74.4 0.9 %reshape.11 = bf16[4,256,256]{2,1,0:T(8,128)(2,1)} reshape(bf16[4,32,2,4,256]{4,3,2,1,0:T(4,128)(2,1)S(1)} %copy.19) | data formatting | bytes 1048576 | tf_op jit(solution)/shard_map/reshape | solution.py:402
  75.3 0.1 copy-done
  75.4 0.8 %copy.21 = bf16[8,256,128]{2,1,0:T(8,128)(2,1)} copy(bf16[8,256,128]{2,1,0:T(8,128)(2,1)S(1)} %copy-done) | data formatting | bytes 1048576
Async XLA Ops:
  74.4 1.1 %copy-start = (bf16[8,256,128]{2,1,0:T(8,128)(2,1)S(1)}, bf16[8,256,128]{2,1,0:T(8,128)(2,1)}, u32[]{:S(2)}) copy-start(bf16[8,256,128]{2,1,0:T(8,128)(2,1)} %get-tuple-element.9) | copy-start | bytes 1572868
where the time goes:
time: 76.5 us; the launch traced here: 76.2 us
  Pallas kernels  72.4 us (95%)
  local copies, waits for them, and re-layouts  3.2 us (4%)
    pallas_call x1, Pallas kernels, body(): pl.pallas_call(functools.partial(kernel, n), out_shape=(jax.ShapeDtypeStr...  72.4 us

commit v1 on v0

v1 whole, which is shorter than its diff:
```python
import functools
import math

import jax
import jax.numpy as jnp
from jax import lax
from jax.experimental import pallas as pl
from jax.experimental.pallas import tpu as pltpu
from jax.sharding import PartitionSpec as P

HEADS = 8
HEAD = 32
C_OPM = 32
LOG2E = math.log2(math.e)
SCALE = LOG2E / math.sqrt(HEAD)
MASKED = -1000000000.0 * LOG2E
NT = (((1,), (1,)), ((), ()))
MESH = pl.DeviceIdType.MESH
VMEM = pl.BlockSpec(memory_space=pltpu.VMEM)
LIMIT = 60 * 1024 * 1024
narrow, full = jnp.bfloat16, jnp.float32


def norm(wide, gain):
    average = jnp.mean(wide, axis=-1, keepdims=True)
    centred = wide - average
    spread = jnp.mean(centred * centred, axis=-1, keepdims=True)
    return (centred * lax.rsqrt(spread + 1e-05) * gain).astype(narrow)


def dot(a, b):
    return jnp.dot(a, b, preferred_element_type=full)


def dot_nt(a, b):
    return lax.dot_general(a, b, NT, preferred_element_type=full)


def flip(b, bit):
    return b + bit - 2 * bit * lax.rem(b // bit, 2)


class Place:
    def __init__(self, me):
        self.me, self.core = me, lax.rem(me, 2)
        self.far, self.near = flip(me, 16), flip(me, 8)
        self.partners = (self.f(me), self.g(me), flip(me, 1), self.far, self.near)

    def f(self, b):
        x, y = 2 - 4 * lax.rem(b // 2, 2), 4 - 8 * lax.rem(b // 4, 2)
        return b + (1 - self.core) * x + self.core * y

    def g(self, b):
        x, y = 2 - 4 * lax.rem(b // 2, 2), 4 - 8 * lax.rem(b // 4, 2)
        return b + self.core * x + (1 - self.core) * y

    def layer(self, b, d):
        if d % 2:
            b = flip(b, 16)
        return flip(b, 8) if d >= 2 else b


def greet(place):
    barrier = pltpu.get_barrier_semaphore()
    for target in place.partners:
        pl.semaphore_signal(barrier, inc=1, device_id={"dap": target}, device_id_type=MESH)


def met(place):
    pl.semaphore_wait(pltpu.get_barrier_semaphore(), len(place.partners))


class Gather:
    def __init__(self, place, out, sems):
        self.place, self.out, self.sems = place, out, sems
        self.sends = []

    def copy(self, kind, slot, block, target):
        return pltpu.make_async_remote_copy(
            src_ref=self.out.at[block],
            dst_ref=self.out.at[block],
            send_sem=self.sems[2 * kind].at[slot],
            recv_sem=self.sems[2 * kind + 1].at[slot],
            device_id={"dap": target},
            device_id_type=MESH,
        )

    def send(self, kind, slot, block, target):
        copy = self.copy(kind, slot, block, target)
        copy.start()
        self.sends.append(copy)

    def to_z(self, slot, block, target):
        self.send(0, slot, block, target)

    def to_f(self, d):
        p = self.place
        self.send(1, d, p.layer(p.me, d), p.f(p.me))

    def to_g(self, d, second):
        p = self.place
        block = p.layer(p.f(p.me) if second else p.me, d)
        self.send(2, d + 4 * second, block, p.g(p.me))

    def to_core(self, d, kind):
        p = self.place
        self.send(3, d + 4 * kind, self.mine(d, kind), flip(p.me, 1))

    def mine(self, d, kind):
        p = self.place
        b = p.me
        if kind % 2:
            b = p.f(b)
        if kind >= 2:
            b = p.g(b)
        return p.layer(b, d)

    def theirs(self, d, kind):
        p = self.place
        b = flip(p.me, 1)
        if kind % 2:
            b = p.g(b)
        if kind >= 2:
            b = p.f(b)
        return p.layer(b, d)

    def got(self, kind, slot, block):
        self.copy(kind, slot, block, flip(self.place.me, 1)).wait_recv()

    def start(self):
        p = self.place
        self.to_z(0, p.me, p.far)
        self.to_z(1, p.me, p.near)
        self.layer_out(0)

    def layer_out(self, d):
        self.to_f(d)
        self.to_g(d, 0)
        self.to_core(d, 0)

    def from_f(self, d):
        self.got(1, d, self.mine(d, 1))
        self.to_g(d, 1)
        self.to_core(d, 1)

    def from_g(self, d):
        self.got(2, d, self.mine(d, 2))
        self.to_core(d, 2)
        self.got(2, d + 4, self.mine(d, 3))
        self.to_core(d, 3)

    def steps(self):
        p = self.place
        self.got(0, 0, p.far)
        self.to_z(2, p.far, p.near)
        self.layer_out(1)
        yield
        self.got(0, 1, p.near)
        self.layer_out(2)
        self.from_f(0)
        yield
        self.got(0, 2, flip(p.near, 16))
        self.layer_out(3)
        self.from_f(1)
        yield
        self.from_f(2)
        self.from_g(0)
        yield
        self.from_f(3)
        self.from_g(1)
        yield
        self.from_g(2)
        yield
        self.from_g(3)
        yield

    def finish(self):
        for kind in range(4):
            for d in range(4):
                self.got(3, d + 4 * kind, self.theirs(d, kind))

    def sent(self):
        for copy in self.sends:
            copy.wait_send()


GATHER = (3, 3, 4, 4, 8, 8, 16, 16)


def gather_sems():
    return [pltpu.SemaphoreType.DMA((size,)) for size in GATHER]


class Exchange:
    def __init__(self, n, me, src, dst, piece, send, recv):
        self.n, self.me, self.src, self.dst = n, me, src, dst
        self.rows, self.first = pl.ds(piece * 16, 16), piece * n
        self.send, self.recv = send, recv

    def copy(self, k, block_out, block_in):
        return pltpu.make_async_remote_copy(
            src_ref=self.src.at[block_out, self.rows],
            dst_ref=self.dst.at[block_in, self.rows],
            send_sem=self.send.at[self.first + k],
            recv_sem=self.recv.at[self.first + k],
            device_id={"dap": block_out},
            device_id_type=MESH,
        )

    def start(self):
        def one(k, carry):
            self.copy(k, lax.rem(self.me + k, self.n), self.me).start()
            return carry

        lax.fori_loop(1, self.n, one, 0)
        self.dst[self.me, self.rows] = self.src[self.me, self.rows]

    def finish(self):
        def one(k, carry):
            target = lax.rem(self.me + k, self.n)
            self.copy(k, target, lax.rem(self.me + self.n - k, self.n)).wait_recv()
            return carry

        lax.fori_loop(1, self.n, one, 0)

    def sent(self):
        def one(k, carry):
            self.copy(k, lax.rem(self.me + k, self.n), self.me).wait_send()
            return carry

        lax.fori_loop(1, self.n, one, 0)


def iotas(rows, columns):
    shape = (rows, columns)
    return lax.broadcasted_iota(jnp.int32, shape, 0), lax.broadcasted_iota(jnp.int32, shape, 1)


def ones_where(condition):
    return condition.astype(full).astype(narrow)


def softmax(scores):
    powers = jnp.exp2(scores - jnp.max(scores, axis=-1, keepdims=True))
    return (powers * (1.0 / jnp.sum(powers, axis=-1, keepdims=True))).astype(narrow)


def attend(joint, gated, keeps, width):
    queries, keys_all = joint[:, :width], joint[:, width:]
    values_all, gates = gated[:, :width], gated[:, width:]
    groups = len(keeps)
    length = joint.shape[0] // groups
    lanes = lax.broadcasted_iota(jnp.int32, (1, width), 1) // HEAD
    totals = [None] * groups
    for h in range(HEADS):
        mine = ones_where(lanes == h)
        asked, given = queries * mine, values_all * mine
        for g in range(groups):
            part = slice(g * length, (g + 1) * length)
            scores = dot_nt(asked[part], keys_all[part]) * SCALE
            weights = softmax(jnp.where(keeps[g], scores, MASKED))
            mixed = dot(weights, given[part])
            totals[g] = mixed if totals[g] is None else totals[g] + mixed
    total = jnp.concatenate(totals, axis=0)
    return (total * jax.nn.sigmoid(gates.astype(full))).astype(narrow)


N_IN = 17


def kernel(n, *refs):
    inputs, (new_alignment, new_pair), scratch = refs[:N_IN], refs[N_IN : N_IN + 2], refs[N_IN + 2 :]
    held, scratch = scratch[:N_IN], scratch[N_IN:]
    (
        bias_a, bias_b, wide_bias, joints, asked_all, gate_all, mixed_all, residual, spread_a,
        spread_b, back_a, back_b, sent, columns, new_sent, back, left, right_a, right_b,
        wide_right, products, wide_output, turned_output, in_sems,
        to_send, to_recv, back_send, back_recv, *sems,
    ) = scratch
    (
        alignment, pair_rep, align_mask, residue_mask, row_gain, pair_gain, row_bias, row_scoring,
        row_values, row_output, column_gain, column_scoring, column_values, column_output,
        outer_gain, outer_inputs, outer_output,
    ) = held
    me = lax.axis_index("dap")
    place = Place(me)
    seqs, total_res, width = alignment.shape
    rows = pair_rep.shape[0]
    channels = pair_rep.shape[2]
    total_seqs = seqs * n
    half = rows // 2
    block = seqs * half

    order = (1, 5, 6, 2, 0, 4, 7, 8, 3, 9, 10, 11, 12, 13, 14, 15, 16)
    loads = [pltpu.make_async_copy(inputs[k], held[k], in_sems.at[k]) for k in range(N_IN)]
    for k in order:
        loads[k].start()
    greet(place)

    for k in (1, 5, 6, 2):
        loads[k].wait()
    biases = []
    for i in range(rows):
        normed = norm(pair_rep[i].astype(full), pair_gain[...])
        biases.append(dot_nt(row_bias[...], normed))
    biases = jnp.concatenate(biases, axis=0).astype(narrow)
    r, c = iotas(rows * HEADS, rows * HEADS)
    piece_of, rest = r // (half * HEADS), r % (half * HEADS)
    biases = dot(ones_where(c == (piece_of * half + rest % half) * HEADS + rest // half), biases).astype(narrow)
    bias_a[me] = biases[: half * HEADS]
    bias_b[me, : half * HEADS] = biases[half * HEADS :]
    mask_rows = jnp.concatenate([align_mask[...].astype(full), jnp.zeros((16 - seqs, total_res), full)], axis=0)
    bias_b[me, half * HEADS :] = mask_rows.astype(narrow)
    met(place)
    gather_a = Gather(place, bias_a, sems[:8])
    gather_b = Gather(place, bias_b, sems[8:16])
    gather_a.start()
    gather_b.start()
    steps_a, steps_b = gather_a.steps(), gather_b.steps()

    for k in (0, 4, 7, 8):
        loads[k].wait()
    r, c = iotas(total_res, total_res)
    lane_head = c // HEAD
    row_half = r % rows // half
    pair_masks = [ones_where(lane_head == 2 * hp + row_half) for hp in range(HEADS // 2)]
    doubles = [ones_where(c == r // rows * rows + piece * half + r % half) for piece in range(2)]

    def project(s):
        normed = norm(alignment[s].astype(full), row_gain[...])
        joint = dot(normed, row_scoring[...]).astype(narrow)
        gated = dot(normed, row_values[...]).astype(narrow)
        joints[s, :, :width] = joint[:, width:]
        joints[s, :, width:] = gated[:, :width]
        for piece in range(2):
            asked_all[piece, s] = dot(doubles[piece], joint[:, :width]).astype(narrow)
            gate_all[piece, s] = jax.nn.sigmoid(dot(doubles[piece], gated[:, width:]))

    for s in range(seqs):
        project(s)
        next(steps_a, None)
        if s > 0:
            next(steps_b, None)
    for k in (3, 9, 10, 11, 12, 13, 14, 15, 16):
        loads[k].wait()

    r, c = iotas(n * block, seqs * total_res)
    same = (r % block // half == c // total_res) & (r // block == c % total_res // rows) & (r % half == c % half)
    spread_a[...] = ones_where(same & (c % rows < half))
    spread_b[...] = ones_where(same & (c % rows >= half))
    spreads = (spread_a, spread_b)
    next(steps_a, None)
    next(steps_b, None)
    flat_alignment = alignment[...].reshape(seqs * total_res, width)
    for piece in range(2):
        residual[piece] = dot(spreads[piece][...], flat_alignment)
    next(steps_a, None)
    next(steps_b, None)
    r, c = iotas(seqs * total_res, n * block)
    same = (c % block // half == r // total_res) & (c // block == r % total_res // rows) & (c % half == r % half)
    back_a[...] = ones_where(same & (r % rows < half))
    back_b[...] = ones_where(same & (r % rows >= half))
    for _ in steps_a:
        next(steps_b, None)

    wide_output[...] = outer_output[...].astype(full).reshape(wide_output.shape)
    for g in range(C_OPM // 8):
        for parity in range(2):
            block_of = [wide_output[:, 2 * (g * 4 + t) + parity, :] for t in range(4)]
            turned_output[parity * channels : (parity + 1) * channels, g * 128 : (g + 1) * 128] = (
                jnp.concatenate(block_of, axis=0).T.astype(narrow)
            )
    gather_a.finish()

    residue_float = residue_mask[...].astype(full)
    bias_blocks = (bias_a, bias_b)
    keeps = [align_mask[s : s + 1, :].astype(full) * residue_float > 0 for s in range(seqs)]

    def row_piece(piece, between):
        wide_bias[...] = bias_blocks[piece][:, : half * HEADS, :].astype(full) * LOG2E
        for s in range(seqs):
            keys_all, values_all = joints[s, :, :width], joints[s, :, width:]
            total = None
            for hp in range(HEADS // 2):
                asked = asked_all[piece, s] * pair_masks[hp]
                bias = wide_bias[:, hp * rows : (hp + 1) * rows, :].reshape(total_res, total_res)
                scores = dot_nt(asked, keys_all) * SCALE + bias
                weights = softmax(jnp.where(keeps[s], scores, MASKED))
                mixed = dot(weights, values_all) * pair_masks[hp].astype(full)
                total = mixed if total is None else total + mixed
            mixed_all[s * total_res : (s + 1) * total_res, :] = (total * gate_all[piece, s]).astype(narrow)
            between()
        mixed = dot(spread_a[...], mixed_all[...]) + dot(spread_b[...], mixed_all[...])
        updated = residual[piece] + dot(mixed.astype(narrow), row_output[...])
        sent[:, piece * block : (piece + 1) * block, :] = updated.astype(narrow).reshape(n, block, width)
        exchange = Exchange(n, me, sent, columns, piece, to_send, to_recv)
        exchange.start()
        return exchange

    def relay_b():
        next(steps_b, None)
        next(steps_b, None)

    to_a = row_piece(0, relay_b)
    for _ in steps_b:
        pass
    gather_b.finish()
    to_b = row_piece(1, lambda: None)

    every_mask = bias_b[:, half * HEADS :, :].reshape(n * 16, total_res)
    r, c = iotas(total_seqs, n * 16)
    mask = dot(ones_where(c == r // seqs * 16 + r % seqs), every_mask).astype(narrow)
    r, c = iotas(rows, total_res)
    own = ones_where(c == me * rows + r)
    keep_columns = dot_nt(own, mask)
    row_factor = jnp.sum(own.astype(full) * residue_float, axis=-1, keepdims=True)
    pair_count = dot(keep_columns.astype(narrow), mask)
    scale = row_factor * residue_float / (0.001 + pair_count)

    length = half * total_seqs
    r, c = iotas(length, length)
    into = ones_where(c == r % total_seqs * half + r // total_seqs)
    out_of = ones_where(r == c % total_seqs * half + c // total_seqs)
    r, c = iotas(C_OPM * half, C_OPM * half)
    by_channel = ones_where(c == r % half * C_OPM + r // half)
    rights = (right_a, right_b)

    def column_piece(piece):
        rows_here = pl.ds(piece * block, block)
        stream = dot(into, columns[:, rows_here].reshape(length, width))
        normed = norm(stream, column_gain[...])
        joint = dot(normed, column_scoring[...]).astype(narrow)
        gated = dot(normed, column_values[...]).astype(narrow)
        mine = range(piece * half, (piece + 1) * half)
        mixed = attend(joint, gated, [keep_columns[i : i + 1, :] > 0 for i in mine], width)
        second = (stream + dot(mixed, column_output[...])).astype(narrow)
        outer_normed = norm(second.astype(full), outer_gain[...])
        right = []
        for t, i in enumerate(mine):
            part = slice(t * total_seqs, (t + 1) * total_seqs)
            sides = dot_nt(outer_inputs[...], outer_normed[part]) * keep_columns[i : i + 1, :]
            left[i] = sides[:C_OPM].astype(narrow)
            right.append(sides[C_OPM:].astype(narrow))
        rights[piece][me] = dot(by_channel, jnp.concatenate(right, axis=0)).astype(narrow)
        gather = Gather(place, rights[piece], sems[16 + 8 * piece : 24 + 8 * piece])
        gather.start()
        new_sent[:, rows_here] = dot(out_of, second).astype(narrow).reshape(n, block, width)
        exchange = Exchange(n, me, new_sent, back, piece, back_send, back_recv)
        exchange.start()
        return gather, exchange

    to_a.finish()
    right_a_gather, home_a = column_piece(0)
    steps_a = right_a_gather.steps()
    for _ in steps_a:
        pass
    to_b.finish()
    right_b_gather, home_b = column_piece(1)
    right_a_gather.finish()
    steps_b = right_b_gather.steps()

    sides = left[...].reshape(rows * C_OPM, total_seqs)

    def outer(piece):
        wide_right[...] = rights[piece][...].astype(full)
        for e in range(C_OPM // 2):
            some = wide_right[:, e * rows : (e + 1) * rows, :].reshape(total_res, total_seqs)
            product = dot_nt(sides, some.astype(narrow)).astype(narrow)
            products[piece, :, e * C_OPM : (e + 1) * C_OPM, :] = product.reshape(rows, C_OPM, total_res)

    next(steps_b, None)
    next(steps_b, None)
    next(steps_b, None)
    outer(0)
    for _ in steps_b:
        pass
    home_a.finish()
    flat_a = dot(back_a[...], back[:, :block].reshape(n * block, width))
    new_alignment[...] = flat_a.astype(narrow).reshape(new_alignment.shape)
    right_b_gather.finish()
    outer(1)
    low = lax.broadcasted_iota(jnp.int32, (1, total_res), 1) % rows < half
    for i in range(rows):
        first = dot(turned_output[...], products[0, i])
        second = dot(turned_output[...], products[1, i])
        kept = jnp.where(low, first[:channels], second[channels:])
        moved = jnp.where(
            low,
            pltpu.roll(first[channels:], total_res - half, 1),
            pltpu.roll(second[:channels], half, 1),
        )
        flat = (kept + moved) * scale[i : i + 1, :]
        new_pair[i] = (pair_rep[i].astype(full) + flat.T).astype(narrow)
    home_b.finish()
    flat_b = dot(back_b[...], back[:, block:].reshape(n * block, width))
    new_alignment[...] = (new_alignment[...].astype(full) + flat_b.reshape(new_alignment.shape)).astype(narrow)
    for exchange in (to_a, to_b, home_a, home_b):
        exchange.sent()
    for gather in (gather_a, gather_b, right_a_gather, right_b_gather):
        gather.sent()


def body(n, alignment, pair_rep, align_mask, residue_mask, *rest):
    (
        row_gain, pair_gain, row_bias, row_scoring, row_values, row_output, column_gain,
        column_scoring, column_values, column_output, outer_gain, outer_inputs, outer_output,
    ) = rest
    seqs, total_res, width = alignment.shape
    rows, _, channels = pair_rep.shape
    total_seqs = seqs * n
    half = rows // 2
    arguments = (
        alignment, pair_rep, align_mask, residue_mask[None], row_gain[None], pair_gain[None],
        row_bias.T, row_scoring, row_values, row_output, column_gain[None], column_scoring,
        column_values, column_output, outer_gain[None], outer_inputs.T, outer_output,
    )
    dma = pltpu.SemaphoreType.DMA
    blocks = (n, seqs * rows, width)
    sent = n * seqs * half
    right_shape = (n, C_OPM * half, total_seqs)
    return pl.pallas_call(
        functools.partial(kernel, n),
        out_shape=(
            jax.ShapeDtypeStruct(alignment.shape, narrow),
            jax.ShapeDtypeStruct(pair_rep.shape, narrow),
        ),
        in_specs=[pl.BlockSpec(memory_space=pltpu.HBM)] * N_IN,
        out_specs=(VMEM, VMEM),
        scratch_shapes=[pltpu.VMEM(array.shape, array.dtype) for array in arguments]
        + [
            pltpu.VMEM((n, HEADS * half, total_res), narrow),
            pltpu.VMEM((n, HEADS * half + 16, total_res), narrow),
            pltpu.VMEM((n, HEADS * half, total_res), full),
            pltpu.VMEM((seqs, total_res, 2 * width), narrow),
            pltpu.VMEM((2, seqs, total_res, width), narrow),
            pltpu.VMEM((2, seqs, total_res, width), full),
            pltpu.VMEM((seqs * total_res, width), narrow),
            pltpu.VMEM((2, sent, width), full),
            pltpu.VMEM((sent, seqs * total_res), narrow),
            pltpu.VMEM((sent, seqs * total_res), narrow),
            pltpu.VMEM((seqs * total_res, sent), narrow),
            pltpu.VMEM((seqs * total_res, sent), narrow),
            pltpu.VMEM(blocks, narrow),
            pltpu.VMEM(blocks, narrow),
            pltpu.VMEM(blocks, narrow),
            pltpu.VMEM(blocks, narrow),
            pltpu.VMEM((rows, C_OPM, total_seqs), narrow),
            pltpu.VMEM(right_shape, narrow),
            pltpu.VMEM(right_shape, narrow),
            pltpu.VMEM(right_shape, full),
            pltpu.VMEM((2, rows, C_OPM * C_OPM // 2, total_res), narrow),
            pltpu.VMEM((C_OPM, C_OPM, channels), full),
            pltpu.VMEM((2 * channels, C_OPM * C_OPM // 2), narrow),
            dma((N_IN,)),
        ]
        + [dma((2 * n,))] * 4
        + gather_sems() * 4,
        compiler_params=pltpu.CompilerParams(
            vmem_limit_bytes=LIMIT, collective_id=0, has_side_effects=True
        ),
        name="evoformer",
    )(*arguments)


def solution(mesh):
    split = P(("dp", "dap"), None, None)
    in_specs = (split, split, P(("dp", "dap"), None), P("dp")) + (P(),) * 13
    return jax.shard_map(
        functools.partial(body, mesh.shape["dap"]),
        mesh=mesh,
        in_specs=in_specs,
        out_specs=(split, split),
        check_vma=False,
    )
```

time: 76.5 us -> 84.2 us (1.10)
  Pallas kernels: 72.4 us -> 80.6 us
    pallas_call x1, Pallas kernels: 72.4 us -> 80.6 us  [body(): pl.pallas_call(functools.partial(kernel, n), out_shape=(jax.ShapeDtypeStr...]
    reshape x2 -> x0, local copies, waits for them, and re-layouts: 2.08 us -> none  [the longest x1 1.17 us: body(): back = back.reshape(n, 2, seqs, rows // 2, width).transpose(2, 0, 1, 3, 4)]
    unnamed x3 -> x4, local copies, waits for them, and re-layouts: 0.93 us -> 2.72 us
where the time goes in v1:
time: 84.2 us; the launch traced here: 84 us
  Pallas kernels  80.6 us (96%)
  local copies, waits for them, and re-layouts  2.72 us (3%)
    pallas_call x1, Pallas kernels, body(): pl.pallas_call(functools.partial(kernel, n), out_shape=(jax.ShapeDtypeStr...  80.6 us
    unnamed x4, local copies, waits for them, and re-layouts  2.72 us

profile of v1, /device:TPU:0, one launch (start us, length us, event | category | flops | bytes accessed | tf_op | source)
XLA Modules:
  0.0 84.0 jit_solution(2603568460337044912)
XLA Ops:
  0.6 80.6 %evoformer.1 = (bf16[4,256,256]{2,1,0:T(8,128)(2,1)}, bf16[8,256,128]{2,1,0:T(8,128)(2,1)}) custom-call(bf16[4,256,256]{2,1,0:T(8,128)(2,1)} %refs_0_.1, bf16[8,256,128]{2,1,0:T(8,128)(2,1)} %refs_1_.1, s32[4,256]{1,0:T(4,128)} %refs_2_.1, s32[1,256]{1,0:T(1,128)} %bitcast.9, f32[1,256]{1,0:T(1,128)} %bitcast.10, f32[1,128]{1,0:T(1,128)} %bitcast.13, ...), custom_call_target="tpu_custom_call" | custom-call | tf_op jit(solution)/shard_map/evoformer/pallas_call | solution.py:521
  81.3 0.0 copy-start
  81.3 1.9 %copy.21 = bf16[4,256,256]{2,1,0:T(8,128)(2,1)} copy(bf16[4,256,256]{2,1,0:T(8,128)(2,1)} %get-tuple-element.4) | data formatting | bytes 1048576
  83.2 0.0 copy-done
  83.2 0.8 copy.22
Async XLA Ops:
  81.3 1.9 %copy-start = (bf16[8,256,128]{2,1,0:T(8,128)(2,1)S(1)}, bf16[8,256,128]{2,1,0:T(8,128)(2,1)}, u32[]{:S(2)}) copy-start(bf16[8,256,128]{2,1,0:T(8,128)(2,1)} %get-tuple-element.5) | copy-start | bytes 1572868

commit v2 on v1

--- a/solution.py
+++ b/solution.py
@@ -42,17 +42,19 @@
 
 class Place:
     def __init__(self, me):
-        self.me, self.core = me, lax.rem(me, 2)
-        self.far, self.near = flip(me, 16), flip(me, 8)
-        self.partners = (self.f(me), self.g(me), flip(me, 1), self.far, self.near)
-
-    def f(self, b):
-        x, y = 2 - 4 * lax.rem(b // 2, 2), 4 - 8 * lax.rem(b // 4, 2)
-        return b + (1 - self.core) * x + self.core * y
-
-    def g(self, b):
-        x, y = 2 - 4 * lax.rem(b // 2, 2), 4 - 8 * lax.rem(b // 4, 2)
-        return b + self.core * x + (1 - self.core) * y
+        self.me, self.other, self.core = me, flip(me, 1), lax.rem(me, 2)
+        self.partners = [self.layer(me, d) for d in (1, 2, 3)] + [self.plane(me, k) for k in (1, 2, 3)] + [self.other]
+
+    def plane(self, b, k):
+        if k % 2:
+            b = flip(b, 2)
+        return flip(b, 4) if k >= 2 else b
+
+    def turn(self, b, k, core):
+        x, y = flip(b, 2) - b, flip(b, 4) - b
+        if k % 2:
+            b = b + (1 - core) * x + core * y
+        return b + core * x + (1 - core) * y if k >= 2 else b
 
     def layer(self, b, d):
         if d % 2:
@@ -71,8 +73,9 @@
 
 
 class Gather:
-    def __init__(self, place, out, sems):
+    def __init__(self, place, out, sems, z_relay, p_relay):
         self.place, self.out, self.sems = place, out, sems
+        self.z_relay, self.p_relay = z_relay, p_relay
         self.sends = []
 
     def copy(self, kind, slot, block, target):
@@ -90,105 +93,78 @@
         copy.start()
         self.sends.append(copy)
 
-    def to_z(self, slot, block, target):
-        self.send(0, slot, block, target)
-
-    def to_f(self, d):
+    def got(self, kind, slot, block):
+        self.copy(kind, slot, block, self.place.other).wait_recv()
+
+    def mine(self, d, k):
+        return self.place.layer(self.spot(self.place.me, k, self.place.core), d)
+
+    def theirs(self, d, k):
+        return self.place.layer(self.spot(self.place.other, k, 1 - self.place.core), d)
+
+    def spot(self, b, k, core):
+        return self.place.turn(b, k, core) if self.p_relay else self.place.plane(b, k)
+
+    def layer_out(self, d):
         p = self.place
-        self.send(1, d, p.layer(p.me, d), p.f(p.me))
-
-    def to_g(self, d, second):
-        p = self.place
-        block = p.layer(p.f(p.me) if second else p.me, d)
-        self.send(2, d + 4 * second, block, p.g(p.me))
-
-    def to_core(self, d, kind):
-        p = self.place
-        self.send(3, d + 4 * kind, self.mine(d, kind), flip(p.me, 1))
-
-    def mine(self, d, kind):
-        p = self.place
-        b = p.me
-        if kind % 2:
-            b = p.f(b)
-        if kind >= 2:
-            b = p.g(b)
-        return p.layer(b, d)
-
-    def theirs(self, d, kind):
-        p = self.place
-        b = flip(p.me, 1)
-        if kind % 2:
-            b = p.g(b)
-        if kind >= 2:
-            b = p.f(b)
-        return p.layer(b, d)
-
-    def got(self, kind, slot, block):
-        self.copy(kind, slot, block, flip(self.place.me, 1)).wait_recv()
+        for k in (1, 2) if self.p_relay else (1, 2, 3):
+            self.send(1, d * 4 + k, self.mine(d, 0), self.mine(0, k))
+        self.send(2, d * 4, self.mine(d, 0), p.other)
+
+    def from_plane(self, d, ks=(1, 2, 3)):
+        for k in ks:
+            self.got(1, d * 4 + k, self.mine(d, k))
+            if self.p_relay and k == 1:
+                self.send(1, d * 4 + 3, self.mine(d, 1), self.mine(0, 2))
+            self.send(2, d * 4 + k, self.mine(d, k), self.place.other)
 
     def start(self):
         p = self.place
-        self.to_z(0, p.me, p.far)
-        self.to_z(1, p.me, p.near)
+        for d in (1, 2) if self.z_relay else (1, 3, 2):
+            self.send(0, d, p.me, p.layer(p.me, d))
         self.layer_out(0)
-
-    def layer_out(self, d):
-        self.to_f(d)
-        self.to_g(d, 0)
-        self.to_core(d, 0)
-
-    def from_f(self, d):
-        self.got(1, d, self.mine(d, 1))
-        self.to_g(d, 1)
-        self.to_core(d, 1)
-
-    def from_g(self, d):
-        self.got(2, d, self.mine(d, 2))
-        self.to_core(d, 2)
-        self.got(2, d + 4, self.mine(d, 3))
-        self.to_core(d, 3)
 
     def steps(self):
         p = self.place
-        self.got(0, 0, p.far)
-        self.to_z(2, p.far, p.near)
-        self.layer_out(1)
+        if self.z_relay:
+            self.got(0, 1, self.mine(1, 0))
+            self.send(0, 3, self.mine(1, 0), p.layer(p.me, 2))
+            self.layer_out(1)
+            yield
+        self.got(0, 2, self.mine(2, 0))
+        self.layer_out(2)
         yield
-        self.got(0, 1, p.near)
-        self.layer_out(2)
-        self.from_f(0)
+        if not self.z_relay:
+            self.got(0, 1, self.mine(1, 0))
+            self.layer_out(1)
+            yield
+        self.got(0, 3, self.mine(3, 0))
+        self.layer_out(3)
         yield
-        self.got(0, 2, flip(p.near, 16))
-        self.layer_out(3)
-        self.from_f(1)
-        yield
-        self.from_f(2)
-        self.from_g(0)
-        yield
-        self.from_f(3)
-        self.from_g(1)
-        yield
-        self.from_g(2)
-        yield
-        self.from_g(3)
-        yield
+        if self.p_relay:
+            for d in (0, 1, 2, 3):
+                self.from_plane(d, (1,))
+            yield
+            for d in (0, 1, 2, 3):
+                self.from_plane(d, (2, 3))
+                yield
+        else:
+            for d in (0, 2, 1, 3):
+                self.from_plane(d)
+                yield
 
     def finish(self):
-        for kind in range(4):
-            for d in range(4):
-                self.got(3, d + 4 * kind, self.theirs(d, kind))
+        for d in range(4):
+            for k in range(4):
+                self.got(2, d * 4 + k, self.theirs(d, k))
 
     def sent(self):
         for copy in self.sends:
             copy.wait_send()
 
 
-GATHER = (3, 3, 4, 4, 8, 8, 16, 16)
-
-
 def gather_sems():
-    return [pltpu.SemaphoreType.DMA((size,)) for size in GATHER]
+    return [pltpu.SemaphoreType.DMA((size,)) for size in (4, 4, 16, 16, 16, 16)]
 
 
 class Exchange:
@@ -245,24 +221,31 @@
     return (powers * (1.0 / jnp.sum(powers, axis=-1, keepdims=True))).astype(narrow)
 
 
-def attend(joint, gated, keeps, width):
-    queries, keys_all = joint[:, :width], joint[:, width:]
-    values_all, gates = gated[:, :width], gated[:, width:]
+def attend(joint, gated, keeps, width, between):
     groups = len(keeps)
     length = joint.shape[0] // groups
-    lanes = lax.broadcasted_iota(jnp.int32, (1, width), 1) // HEAD
-    totals = [None] * groups
-    for h in range(HEADS):
-        mine = ones_where(lanes == h)
-        asked, given = queries * mine, values_all * mine
-        for g in range(groups):
-            part = slice(g * length, (g + 1) * length)
-            scores = dot_nt(asked[part], keys_all[part]) * SCALE
+    side = width // 2
+    some = HEADS // 2
+    lanes = lax.broadcasted_iota(jnp.int32, (length, side), 1) // HEAD
+    picks = [ones_where(lanes == h) for h in range(some)]
+    totals = []
+    for g in range(groups):
+        part = slice(g * length, (g + 1) * length)
+        sides = []
+        for first in (0, side):
+            queries, keys_all = joint[part, first : first + side], joint[part, width + first : width + first + side]
+            asked = jnp.concatenate([queries * pick for pick in picks], axis=0)
+            scores = dot_nt(asked, keys_all) * SCALE
             weights = softmax(jnp.where(keeps[g], scores, MASKED))
-            mixed = dot(weights, given[part])
-            totals[g] = mixed if totals[g] is None else totals[g] + mixed
+            mixed = dot(weights, gated[part, first : first + side])
+            total = mixed[:length]
+            for h in range(1, some):
+                total = jnp.where(lanes == h, mixed[h * length : (h + 1) * length], total)
+            sides.append(total)
+            between()
+        totals.append(jnp.concatenate(sides, axis=1))
     total = jnp.concatenate(totals, axis=0)
-    return (total * jax.nn.sigmoid(gates.astype(full))).astype(narrow)
+    return (total * jax.nn.sigmoid(gated[:, width:].astype(full))).astype(narrow)
 
 
 N_IN = 17
@@ -273,8 +256,8 @@
     held, scratch = scratch[:N_IN], scratch[N_IN:]
     (
         bias_a, bias_b, wide_bias, joints, asked_all, gate_all, mixed_all, residual, spread_a,
-        spread_b, back_a, back_b, sent, columns, new_sent, back, left, right_a, right_b,
-        wide_right, products, wide_output, turned_output, in_sems,
+        spread_b, spread_both, back_a, back_b, sent, columns, new_sent, back, left, right_a, right_b,
+        wide_right, products, outer_a, wide_output, turned_output, in_sems,
         to_send, to_recv, back_send, back_recv, *sems,
     ) = scratch
     (
@@ -312,18 +295,18 @@
     mask_rows = jnp.concatenate([align_mask[...].astype(full), jnp.zeros((16 - seqs, total_res), full)], axis=0)
     bias_b[me, half * HEADS :] = mask_rows.astype(narrow)
     met(place)
-    gather_a = Gather(place, bias_a, sems[:8])
-    gather_b = Gather(place, bias_b, sems[8:16])
+    gather_a = Gather(place, bias_a, sems[:6], False, False)
+    gather_b = Gather(place, bias_b, sems[6:12], False, False)
     gather_a.start()
-    gather_b.start()
     steps_a, steps_b = gather_a.steps(), gather_b.steps()
 
     for k in (0, 4, 7, 8):
         loads[k].wait()
     r, c = iotas(total_res, total_res)
-    lane_head = c // HEAD
-    row_half = r % rows // half
-    pair_masks = [ones_where(lane_head == 2 * hp + row_half) for hp in range(HEADS // 2)]
+    lane_head = c[:, : width // 2] // HEAD
+    row_half = r[:, : width // 2] % rows // half
+    kept = [lane_head == 2 * hp + row_half for hp in range(2)]
+    pair_masks = [ones_where(k) for k in kept]
     doubles = [ones_where(c == r // rows * rows + piece * half + r % half) for piece in range(2)]
 
     def project(s):
@@ -338,9 +321,10 @@
 
     for s in range(seqs):
         project(s)
-        next(steps_a, None)
-        if s > 0:
-            next(steps_b, None)
+        if s == 1:
+            for _ in range(3):
+                next(steps_a, None)
+            gather_b.start()
     for k in (3, 9, 10, 11, 12, 13, 14, 15, 16):
         loads[k].wait()
 
@@ -348,20 +332,22 @@
     same = (r % block // half == c // total_res) & (r // block == c % total_res // rows) & (r % half == c % half)
     spread_a[...] = ones_where(same & (c % rows < half))
     spread_b[...] = ones_where(same & (c % rows >= half))
+    spread_both[...] = ones_where(same)
     spreads = (spread_a, spread_b)
     next(steps_a, None)
-    next(steps_b, None)
+    next(steps_a, None)
+    for _ in range(3):
+        next(steps_b, None)
     flat_alignment = alignment[...].reshape(seqs * total_res, width)
     for piece in range(2):
         residual[piece] = dot(spreads[piece][...], flat_alignment)
     next(steps_a, None)
-    next(steps_b, None)
     r, c = iotas(seqs * total_res, n * block)
     same = (c % block // half == r // total_res) & (c // block == r % total_res // rows) & (c % half == r % half)
     back_a[...] = ones_where(same & (r % rows < half))
     back_b[...] = ones_where(same & (r % rows >= half))
     for _ in steps_a:
-        next(steps_b, None)
+        pass
 
     wide_output[...] = outer_output[...].astype(full).reshape(wide_output.shape)
     for g in range(C_OPM // 8):
@@ -380,17 +366,23 @@
         wide_bias[...] = bias_blocks[piece][:, : half * HEADS, :].astype(full) * LOG2E
         for s in range(seqs):
             keys_all, values_all = joints[s, :, :width], joints[s, :, width:]
-            total = None
+            side = width // 2
+            sides = []
             for hp in range(HEADS // 2):
-                asked = asked_all[piece, s] * pair_masks[hp]
+                lanes_here = slice(hp // 2 * side, (hp // 2 + 1) * side)
+                asked = asked_all[piece, s][:, lanes_here] * pair_masks[hp % 2]
                 bias = wide_bias[:, hp * rows : (hp + 1) * rows, :].reshape(total_res, total_res)
-                scores = dot_nt(asked, keys_all) * SCALE + bias
+                scores = dot_nt(asked, keys_all[:, lanes_here]) * SCALE + bias
                 weights = softmax(jnp.where(keeps[s], scores, MASKED))
-                mixed = dot(weights, values_all) * pair_masks[hp].astype(full)
-                total = mixed if total is None else total + mixed
+                mixed = dot(weights, values_all[:, lanes_here])
+                if hp % 2:
+                    sides[-1] = jnp.where(kept[1], mixed, sides[-1])
+                else:
+                    sides.append(jnp.where(kept[0], mixed, 0.0))
+            total = jnp.concatenate(sides, axis=1)
             mixed_all[s * total_res : (s + 1) * total_res, :] = (total * gate_all[piece, s]).astype(narrow)
             between()
-        mixed = dot(spread_a[...], mixed_all[...]) + dot(spread_b[...], mixed_all[...])
+        mixed = dot(spread_both[...], mixed_all[...])
         updated = residual[piece] + dot(mixed.astype(narrow), row_output[...])
         sent[:, piece * block : (piece + 1) * block, :] = updated.astype(narrow).reshape(n, block, width)
         exchange = Exchange(n, me, sent, columns, piece, to_send, to_recv)
@@ -398,7 +390,6 @@
         return exchange
 
     def relay_b():
-        next(steps_b, None)
         next(steps_b, None)
 
     to_a = row_piece(0, relay_b)
@@ -425,14 +416,14 @@
     by_channel = ones_where(c == r % half * C_OPM + r // half)
     rights = (right_a, right_b)
 
-    def column_piece(piece):
+    def column_piece(piece, between):
         rows_here = pl.ds(piece * block, block)
         stream = dot(into, columns[:, rows_here].reshape(length, width))
         normed = norm(stream, column_gain[...])
         joint = dot(normed, column_scoring[...]).astype(narrow)
         gated = dot(normed, column_values[...]).astype(narrow)
         mine = range(piece * half, (piece + 1) * half)
-        mixed = attend(joint, gated, [keep_columns[i : i + 1, :] > 0 for i in mine], width)
+        mixed = attend(joint, gated, [keep_columns[i : i + 1, :] > 0 for i in mine], width, between)
         second = (stream + dot(mixed, column_output[...])).astype(narrow)
         outer_normed = norm(second.astype(full), outer_gain[...])
         right = []
@@ -442,22 +433,23 @@
             left[i] = sides[:C_OPM].astype(narrow)
             right.append(sides[C_OPM:].astype(narrow))
         rights[piece][me] = dot(by_channel, jnp.concatenate(right, axis=0)).astype(narrow)
-        gather = Gather(place, rights[piece], sems[16 + 8 * piece : 24 + 8 * piece])
+        gather = Gather(place, rights[piece], sems[12 + 6 * piece : 18 + 6 * piece], False, False)
         gather.start()
         new_sent[:, rows_here] = dot(out_of, second).astype(narrow).reshape(n, block, width)
+        steps = gather.steps()
+        for _ in range(3):
+            next(steps, None)
         exchange = Exchange(n, me, new_sent, back, piece, back_send, back_recv)
         exchange.start()
-        return gather, exchange
+        return gather, steps, exchange
 
     to_a.finish()
-    right_a_gather, home_a = column_piece(0)
-    steps_a = right_a_gather.steps()
+    right_a_gather, steps_a, home_a = column_piece(0, lambda: None)
+    next(steps_a, None)
+    to_b.finish()
+    right_b_gather, steps_b, home_b = column_piece(1, lambda: None)
     for _ in steps_a:
         pass
-    to_b.finish()
-    right_b_gather, home_b = column_piece(1)
-    right_a_gather.finish()
-    steps_b = right_b_gather.steps()
 
     sides = left[...].reshape(rows * C_OPM, total_seqs)
 
@@ -466,30 +458,27 @@
         for e in range(C_OPM // 2):
             some = wide_right[:, e * rows : (e + 1) * rows, :].reshape(total_res, total_seqs)
             product = dot_nt(sides, some.astype(narrow)).astype(narrow)
-            products[piece, :, e * C_OPM : (e + 1) * C_OPM, :] = product.reshape(rows, C_OPM, total_res)
-
+            products[:, e * C_OPM : (e + 1) * C_OPM, :] = product.reshape(rows, C_OPM, total_res)
+        for i in range(rows):
+            yield i, dot(turned_output[...], products[i])
+
+    low = lax.broadcasted_iota(jnp.int32, (1, total_res), 1) % rows < half
     next(steps_b, None)
-    next(steps_b, None)
-    next(steps_b, None)
-    outer(0)
+    right_a_gather.finish()
+    for i, first in outer(0):
+        moved = pltpu.roll(first[channels:], total_res - half, 1)
+        outer_a[i] = jnp.where(low, first[:channels] + moved, 0.0)
+        if i in (0, 2, 4, 6):
+            next(steps_b, None)
     for _ in steps_b:
         pass
     home_a.finish()
     flat_a = dot(back_a[...], back[:, :block].reshape(n * block, width))
     new_alignment[...] = flat_a.astype(narrow).reshape(new_alignment.shape)
     right_b_gather.finish()
-    outer(1)
-    low = lax.broadcasted_iota(jnp.int32, (1, total_res), 1) % rows < half
-    for i in range(rows):
-        first = dot(turned_output[...], products[0, i])
-        second = dot(turned_output[...], products[1, i])
-        kept = jnp.where(low, first[:channels], second[channels:])
-        moved = jnp.where(
-            low,
-            pltpu.roll(first[channels:], total_res - half, 1),
-            pltpu.roll(second[:channels], half, 1),
-        )
-        flat = (kept + moved) * scale[i : i + 1, :]
+    for i, second in outer(1):
+        moved = pltpu.roll(second[:channels], half, 1)
+        flat = (outer_a[i] + jnp.where(low, 0.0, second[channels:] + moved)) * scale[i : i + 1, :]
         new_pair[i] = (pair_rep[i].astype(full) + flat.T).astype(narrow)
     home_b.finish()
     flat_b = dot(back_b[...], back[:, block:].reshape(n * block, width))
@@ -538,6 +527,7 @@
             pltpu.VMEM((2, sent, width), full),
             pltpu.VMEM((sent, seqs * total_res), narrow),
             pltpu.VMEM((sent, seqs * total_res), narrow),
+            pltpu.VMEM((sent, seqs * total_res), narrow),
             pltpu.VMEM((seqs * total_res, sent), narrow),
             pltpu.VMEM((seqs * total_res, sent), narrow),
             pltpu.VMEM(blocks, narrow),
@@ -548,7 +538,8 @@
             pltpu.VMEM(right_shape, narrow),
             pltpu.VMEM(right_shape, narrow),
             pltpu.VMEM(right_shape, full),
-            pltpu.VMEM((2, rows, C_OPM * C_OPM // 2, total_res), narrow),
+            pltpu.VMEM((rows, C_OPM * C_OPM // 2, total_res), narrow),
+            pltpu.VMEM((rows, channels, total_res), full),
             pltpu.VMEM((C_OPM, C_OPM, channels), full),
             pltpu.VMEM((2 * channels, C_OPM * C_OPM // 2), narrow),
             dma((N_IN,)),

time: 84.2 us -> 68.8 us (0.82)
  Pallas kernels: 80.6 us -> 65.3 us
    pallas_call x1, Pallas kernels: 80.6 us -> 65.3 us  [body(): pl.pallas_call(functools.partial(kernel, n), out_shape=(jax.ShapeDtypeStr...]
where the time goes in v2:
time: 68.8 us; the launch traced here: 68.7 us
  Pallas kernels  65.3 us (95%)
  local copies, waits for them, and re-layouts  2.72 us (4%)
    pallas_call x1, Pallas kernels, body(): pl.pallas_call(functools.partial(kernel, n), out_shape=(jax.ShapeDtypeStr...  65.3 us
    unnamed x4, local copies, waits for them, and re-layouts  2.72 us

profile of v2, /device:TPU:0, one launch (start us, length us, event | category | flops | bytes accessed | tf_op | source)
XLA Modules:
  0.0 68.7 jit_solution(6418681044879468378)
XLA Ops:
  0.6 65.3 %evoformer.1 = (bf16[4,256,256]{2,1,0:T(8,128)(2,1)}, bf16[8,256,128]{2,1,0:T(8,128)(2,1)}) custom-call(bf16[4,256,256]{2,1,0:T(8,128)(2,1)} %refs_0_.1, bf16[8,256,128]{2,1,0:T(8,128)(2,1)} %refs_1_.1, s32[4,256]{1,0:T(4,128)} %refs_2_.1, s32[1,256]{1,0:T(1,128)} %bitcast.9, f32[1,256]{1,0:T(1,128)} %bitcast.10, f32[1,128]{1,0:T(1,128)} %bitcast.13, ...), custom_call_target="tpu_custom_call" | custom-call | tf_op jit(solution)/shard_map/evoformer/pallas_call | solution.py:510
  66.0 0.0 copy-start
  66.0 1.9 %copy.21 = bf16[4,256,256]{2,1,0:T(8,128)(2,1)} copy(bf16[4,256,256]{2,1,0:T(8,128)(2,1)} %get-tuple-element.4) | data formatting | bytes 1048576
  67.9 0.0 copy-done
  67.9 0.8 %copy.22 = bf16[8,256,128]{2,1,0:T(8,128)(2,1)} copy(bf16[8,256,128]{2,1,0:T(8,128)(2,1)S(1)} %copy-done) | data formatting | bytes 1048576
Async XLA Ops:
  66.0 1.9 %copy-start = (bf16[8,256,128]{2,1,0:T(8,128)(2,1)S(1)}, bf16[8,256,128]{2,1,0:T(8,128)(2,1)}, u32[]{:S(2)}) copy-start(bf16[8,256,128]{2,1,0:T(8,128)(2,1)} %get-tuple-element.5) | copy-start | bytes 1572868

commit v3 on v2

--- a/solution.py
+++ b/solution.py
@@ -169,42 +169,67 @@
 
 class Exchange:
     def __init__(self, n, me, src, dst, piece, send, recv):
-        self.n, self.me, self.src, self.dst = n, me, src, dst
+        self.me, self.src, self.dst, self.half = me, src, dst, n // 2
         self.rows, self.first = pl.ds(piece * 16, 16), piece * n
         self.send, self.recv = send, recv
-
-    def copy(self, k, block_out, block_in):
+        self.home = me // self.half * self.half
+        self.away = self.half - self.home
+
+    def copy(self, base, k, slot):
+        out = base + lax.rem(self.me + k, self.half)
         return pltpu.make_async_remote_copy(
-            src_ref=self.src.at[block_out, self.rows],
-            dst_ref=self.dst.at[block_in, self.rows],
-            send_sem=self.send.at[self.first + k],
-            recv_sem=self.recv.at[self.first + k],
-            device_id={"dap": block_out},
+            src_ref=self.src.at[out, self.rows],
+            dst_ref=self.dst.at[self.me, self.rows],
+            send_sem=self.send.at[slot],
+            recv_sem=self.recv.at[slot],
+            device_id={"dap": out},
             device_id_type=MESH,
         )
 
+    def arrival(self, base, k, slot):
+        come = base + lax.rem(self.me + self.half - k, self.half)
+        return pltpu.make_async_remote_copy(
+            src_ref=self.src.at[come, self.rows],
+            dst_ref=self.dst.at[come, self.rows],
+            send_sem=self.send.at[slot],
+            recv_sem=self.recv.at[slot],
+            device_id={"dap": come},
+            device_id_type=MESH,
+        )
+
+    def each(self, act):
+        def away(k, carry):
+            act(self.away, k, self.first + k)
+            return carry
+
+        def home(k, carry):
+            act(self.home, k, self.first + self.half + k)
+            return carry
+
+        return functools.partial(lax.fori_loop, 0, self.half, away, 0), functools.partial(
+            lax.fori_loop, 1, self.half, home, 0
+        )
+
+    def start_away(self):
+        self.each(lambda *at: self.copy(*at).start())[0]()
+
+    def start_home(self):
+        self.each(lambda *at: self.copy(*at).start())[1]()
+        self.dst[self.me, self.rows] = self.src[self.me, self.rows]
+
     def start(self):
-        def one(k, carry):
-            self.copy(k, lax.rem(self.me + k, self.n), self.me).start()
-            return carry
-
-        lax.fori_loop(1, self.n, one, 0)
-        self.dst[self.me, self.rows] = self.src[self.me, self.rows]
+        self.start_away()
+        self.start_home()
 
     def finish(self):
-        def one(k, carry):
-            target = lax.rem(self.me + k, self.n)
-            self.copy(k, target, lax.rem(self.me + self.n - k, self.n)).wait_recv()
-            return carry
-
-        lax.fori_loop(1, self.n, one, 0)
+        away, home = self.each(lambda *at: self.arrival(*at).wait_recv())
+        home()
+        away()
 
     def sent(self):
-        def one(k, carry):
-            self.copy(k, lax.rem(self.me + k, self.n), self.me).wait_send()
-            return carry
-
-        lax.fori_loop(1, self.n, one, 0)
+        away, home = self.each(lambda *at: self.copy(*at).wait_send())
+        home()
+        away()
 
 
 def iotas(rows, columns):
@@ -249,6 +274,7 @@
 
 
 N_IN = 17
+PARTS = 2
 
 
 def kernel(n, *refs):
@@ -303,8 +329,8 @@
     for k in (0, 4, 7, 8):
         loads[k].wait()
     r, c = iotas(total_res, total_res)
-    lane_head = c[:, : width // 2] // HEAD
-    row_half = r[:, : width // 2] % rows // half
+    lane_head = c[: total_res // 2, : width // 2] // HEAD
+    row_half = r[: total_res // 2, : width // 2] % rows // half
     kept = [lane_head == 2 * hp + row_half for hp in range(2)]
     pair_masks = [ones_where(k) for k in kept]
     doubles = [ones_where(c == r // rows * rows + piece * half + r % half) for piece in range(2)]
@@ -332,12 +358,14 @@
     same = (r % block // half == c // total_res) & (r // block == c % total_res // rows) & (r % half == c % half)
     spread_a[...] = ones_where(same & (c % rows < half))
     spread_b[...] = ones_where(same & (c % rows >= half))
-    spread_both[...] = ones_where(same)
     spreads = (spread_a, spread_b)
     next(steps_a, None)
     next(steps_a, None)
     for _ in range(3):
         next(steps_b, None)
+    r, c = iotas(n * block // 2, seqs * total_res // 2)
+    same = (r % block // half == c // (total_res // 2)) & (r // block == c % (total_res // 2) // rows)
+    spread_both[...] = ones_where(same & (r % half == c % half))
     flat_alignment = alignment[...].reshape(seqs * total_res, width)
     for piece in range(2):
         residual[piece] = dot(spreads[piece][...], flat_alignment)
@@ -362,16 +390,21 @@
     bias_blocks = (bias_a, bias_b)
     keeps = [align_mask[s : s + 1, :].astype(full) * residue_float > 0 for s in range(seqs)]
 
-    def row_piece(piece, between):
-        wide_bias[...] = bias_blocks[piece][:, : half * HEADS, :].astype(full) * LOG2E
+    count = n // 2
+    side = width // 2
+
+    def row_part(piece, base, between):
+        wide = bias_blocks[piece][pl.ds(base, count), : half * HEADS, :].astype(full) * LOG2E
+        wide_bias[...] = wide
+        doubled = pl.ds(pl.multiple_of(base * rows, count * rows), count * rows)
         for s in range(seqs):
             keys_all, values_all = joints[s, :, :width], joints[s, :, width:]
-            side = width // 2
+            queries = asked_all[piece, s, doubled, :]
             sides = []
             for hp in range(HEADS // 2):
                 lanes_here = slice(hp // 2 * side, (hp // 2 + 1) * side)
-                asked = asked_all[piece, s][:, lanes_here] * pair_masks[hp % 2]
-                bias = wide_bias[:, hp * rows : (hp + 1) * rows, :].reshape(total_res, total_res)
+                asked = queries[:, lanes_here] * pair_masks[hp % 2]
+                bias = wide_bias[:, hp * rows : (hp + 1) * rows, :].reshape(count * rows, total_res)
                 scores = dot_nt(asked, keys_all[:, lanes_here]) * SCALE + bias
                 weights = softmax(jnp.where(keeps[s], scores, MASKED))
                 mixed = dot(weights, values_all[:, lanes_here])
@@ -380,13 +413,22 @@
                 else:
                     sides.append(jnp.where(kept[0], mixed, 0.0))
             total = jnp.concatenate(sides, axis=1)
-            mixed_all[s * total_res : (s + 1) * total_res, :] = (total * gate_all[piece, s]).astype(narrow)
+            here = slice(s * count * rows, (s + 1) * count * rows)
+            mixed_all[here, :] = (total * gate_all[piece, s, doubled, :]).astype(narrow)
             between()
-        mixed = dot(spread_both[...], mixed_all[...])
-        updated = residual[piece] + dot(mixed.astype(narrow), row_output[...])
-        sent[:, piece * block : (piece + 1) * block, :] = updated.astype(narrow).reshape(n, block, width)
+        mixed = dot(spread_both[...], mixed_all[...]).astype(narrow)
+        start = pl.multiple_of(base * block, count * block)
+        updated = residual[piece, pl.ds(start, count * block), :] + dot(mixed, row_output[...])
+        sent[pl.ds(base, count), piece * block : (piece + 1) * block, :] = (
+            updated.astype(narrow).reshape(count, block, width)
+        )
+
+    def row_piece(piece, between):
         exchange = Exchange(n, me, sent, columns, piece, to_send, to_recv)
-        exchange.start()
+        row_part(piece, exchange.away, lambda: None)
+        exchange.start_away()
+        row_part(piece, exchange.home, between)
+        exchange.start_home()
         return exchange
 
     def relay_b():
@@ -489,6 +531,25 @@
         gather.sent()
 
 
+def publish(first, second, first_out, second_out, first_held, second_held, arrived, done):
+    ins, outs = [], []
+    for k, (source, held, target) in enumerate(
+        ((first, first_held, first_out), (second, second_held, second_out))
+    ):
+        size = source.shape[0] // PARTS
+        for part in range(PARTS):
+            here = pl.ds(part * size, size)
+            ins.append(pltpu.make_async_copy(source.at[here], held.at[here], arrived.at[k, part]))
+            outs.append(pltpu.make_async_copy(held.at[here], target.at[here], done.at[k, part]))
+    for copy in ins:
+        copy.start()
+    for copy, onward in zip(ins, outs):
+        copy.wait()
+        onward.start()
+    for copy in outs:
+        copy.wait()
+
+
 def body(n, alignment, pair_rep, align_mask, residue_mask, *rest):
     (
         row_gain, pair_gain, row_bias, row_scoring, row_values, row_output, column_gain,
@@ -507,7 +568,7 @@
     blocks = (n, seqs * rows, width)
     sent = n * seqs * half
     right_shape = (n, C_OPM * half, total_seqs)
-    return pl.pallas_call(
+    results = pl.pallas_call(
         functools.partial(kernel, n),
         out_shape=(
             jax.ShapeDtypeStruct(alignment.shape, narrow),
@@ -519,15 +580,15 @@
         + [
             pltpu.VMEM((n, HEADS * half, total_res), narrow),
             pltpu.VMEM((n, HEADS * half + 16, total_res), narrow),
-            pltpu.VMEM((n, HEADS * half, total_res), full),
+            pltpu.VMEM((n // 2, HEADS * half, total_res), full),
             pltpu.VMEM((seqs, total_res, 2 * width), narrow),
             pltpu.VMEM((2, seqs, total_res, width), narrow),
             pltpu.VMEM((2, seqs, total_res, width), full),
-            pltpu.VMEM((seqs * total_res, width), narrow),
+            pltpu.VMEM((seqs * total_res // 2, width), narrow),
             pltpu.VMEM((2, sent, width), full),
             pltpu.VMEM((sent, seqs * total_res), narrow),
             pltpu.VMEM((sent, seqs * total_res), narrow),
-            pltpu.VMEM((sent, seqs * total_res), narrow),
+            pltpu.VMEM((sent // 2, seqs * total_res // 2), narrow),
             pltpu.VMEM((seqs * total_res, sent), narrow),
             pltpu.VMEM((seqs * total_res, sent), narrow),
             pltpu.VMEM(blocks, narrow),
@@ -551,6 +612,14 @@
         ),
         name="evoformer",
     )(*arguments)
+    return pl.pallas_call(
+        publish,
+        out_shape=[jax.ShapeDtypeStruct(array.shape, narrow) for array in results],
+        in_specs=[pl.BlockSpec(memory_space=pl.ANY)] * 2,
+        out_specs=[pl.BlockSpec(memory_space=pl.ANY)] * 2,
+        scratch_shapes=[pltpu.VMEM(array.shape, narrow) for array in results] + [dma((2, PARTS))] * 2,
+        name="publish",
+    )(*results)
 
 
 def solution(mesh):

time: 68.8 us -> 63.1 us (0.917)
  Pallas kernels: 65.3 us -> 62.1 us
  local copies, waits for them, and re-layouts: 2.72 us -> 0 us
    pallas_call x1, Pallas kernels: 65.3 us -> 60.2 us  [body(): pl.pallas_call(functools.partial(kernel, n), out_shape=(jax.ShapeDtypeStr...]
    unnamed x4 -> x0, local copies, waits for them, and re-layouts: 2.72 us -> none
    pallas_call x0 -> x1, Pallas kernels: none -> 1.98 us  [body(): pl.pallas_call(publish, out_shape=[jax.ShapeDtypeStruct(array.shape, narr...]
where the time goes in v3:
time: 63.1 us; the launch traced here: 63 us
  Pallas kernels  62.1 us (98%)
  between operations  0.83 us (1%)
    pallas_call x1, Pallas kernels, body(): pl.pallas_call(functools.partial(kernel, n), out_shape=(jax.ShapeDtypeStr...  60.2 us
    pallas_call x1, Pallas kernels, body(): pl.pallas_call(publish, out_shape=[jax.ShapeDtypeStruct(array.shape, narr...  1.98 us

profile of v3, /device:TPU:0, one launch (start us, length us, event | category | flops | bytes accessed | tf_op | source)
XLA Modules:
  0.0 63.0 jit_solution(6965819872132429374)
XLA Ops:
  0.6 60.2 %evoformer.1 = (bf16[4,256,256]{2,1,0:T(8,128)(2,1)}, bf16[8,256,128]{2,1,0:T(8,128)(2,1)}) custom-call(bf16[4,256,256]{2,1,0:T(8,128)(2,1)} %refs_0_.1, bf16[8,256,128]{2,1,0:T(8,128)(2,1)} %refs_1_.1, s32[4,256]{1,0:T(4,128)} %refs_2_.1, s32[1,256]{1,0:T(1,128)} %bitcast.9, f32[1,256]{1,0:T(1,128)} %bitcast.10, f32[1,128]{1,0:T(1,128)} %bitcast.13, ...), custom_call_target="tpu_custom_call" | custom-call | tf_op jit(solution)/shard_map/evoformer/pallas_call | solution.py:571
  60.8 2.0 %publish.1 = (bf16[4,256,256]{2,1,0:T(8,128)(2,1)}, bf16[8,256,128]{2,1,0:T(8,128)(2,1)}) custom-call(bf16[4,256,256]{2,1,0:T(8,128)(2,1)} %get-tuple-element.4.first, bf16[8,256,128]{2,1,0:T(8,128)(2,1)} %get-tuple-element.5.second), custom_call_target="tpu_custom_call" | custom-call | tf_op jit(solution)/shard_map/publish/pallas_call | solution.py:615
